TPU v7x, 32 devices: a whole 2x2x4 slice. The times are simulated.
32 devices in a mesh: row: 16 (over z, y, x), col: 2 (over core).
Axes of the slice: x: 2, y: 2, z: 4, core: 2. Of those that a mesh axis runs over, the one named last changes fastest.
Arguments:
- points: float32 [8, 8192], P(None, 'row'), may hold values from -6 to 6
- lengthscale: float32 [8], replicated, may hold values from 1 to 3
- noise: float32 [8192], P('row'), may hold values from 0.3 to 3
- target: float32 [8192], P('row'), may hold values from -6 to 6
- probe_bits: int32 [8, 8192], P(None, 'row'), may hold values from 0 to 1
Outputs:
- solution: float32 [9, 8192], P(None, 'row')
- residual: float32 [9, 8192], P(None, 'row')
All inputs are finite; a program needn't handle non-finite values.
Results may differ from a plain program's by a relative error of at most 0.0003.
Values sent between devices are 32-bit elements; how exact they have to be, the bound alone decides.
A program may use at most 64 MiB of HBM per device.

v0:
```python
import jax
import jax.numpy as jnp
from jax import lax
from jax.sharding import PartitionSpec as P

ITERS = 2


root_five = 5.0**0.5


def matern_values(dist_sq):
    scaled_dist = root_five * jnp.sqrt(dist_sq)
    return (1.0 + scaled_dist + scaled_dist * scaled_dist / 3.0) * jnp.exp(-scaled_dist)


def tile_product(row_points, column_points, column_dirs):
    row_count = row_points.shape[1]
    column_count = column_points.shape[1]
    width = min(1024, column_count)
    blocks = column_count // width

    def block_step(index_block, accum):
        column_here = lax.dynamic_slice_in_dim(column_points, index_block * width, width, 1)
        dirs_here = lax.dynamic_slice_in_dim(column_dirs, index_block * width, width, 1)
        dist_sq = jnp.zeros((row_count, width), jnp.float32)
        for feature in range(row_points.shape[0]):
            offset = row_points[feature][:, None] - column_here[feature][None, :]
            dist_sq = dist_sq + offset * offset
        kernel_tile = matern_values(dist_sq)
        return accum + lax.dot_general(
            dirs_here,
            kernel_tile,
            (((1,), (1,)), ((), ())),
            precision=lax.Precision.HIGHEST,
            preferred_element_type=jnp.float32,
        )

    start_value = jnp.zeros((column_dirs.shape[0], row_count), jnp.float32)
    return lax.fori_loop(0, blocks, block_step, start_value)


def row_squares(residual):
    return lax.psum(jnp.sum(residual * residual, axis=1), "row")


def per_device(points, lengthscale, noise, target, probe_bits):
    inverse_scale = 1.0 / lengthscale
    own_points = points * inverse_scale[:, None]
    every_point = lax.all_gather(points, "row", axis=1, tiled=True) * inverse_scale[:, None]
    col_count = lax.axis_size("col")
    col_index = lax.axis_index("col")
    col_width = every_point.shape[1] // col_count
    column_points = lax.dynamic_slice_in_dim(every_point, col_index * col_width, col_width, 1)
    signs = 2.0 * probe_bits.astype(jnp.float32) - 1.0
    rhs = jnp.concatenate([signs, target[None, :]], axis=0)
    solution = jnp.zeros_like(rhs)
    residual = rhs
    direction = rhs
    norm_now = row_squares(residual)
    for iteration in range(ITERS):
        whole_dirs = lax.all_gather(direction, "row", axis=1, tiled=True)
        column_dirs = lax.dynamic_slice_in_dim(whole_dirs, col_index * col_width, col_width, 1)
        partial_image = tile_product(own_points, column_points, column_dirs)
        image = lax.psum(partial_image, "col") + noise[None, :] * direction
        curve = lax.psum(jnp.sum(direction * image, axis=1), "row")
        alpha = norm_now / curve
        solution = solution + alpha[:, None] * direction
        residual = residual - alpha[:, None] * image
        if iteration + 1 < ITERS:
            norm_next = row_squares(residual)
            direction = residual + (norm_next / norm_now)[:, None] * direction
            norm_now = norm_next
    return (solution, residual)


def solution(mesh):
    return jax.shard_map(
        per_device,
        mesh=mesh,
        in_specs=(P(None, "row"), P(), P("row"), P("row"), P(None, "row")),
        out_specs=(P(None, "row"), P(None, "row")),
        check_vma=False,
    )
```

profile of v0, /device:TPU:0, one launch (start us, length us, event | category | flops | bytes accessed | tf_op | source)
XLA Modules:
  0.0 283.0 jit_solution(6453764177039460827)
XLA Ops:
  0.6 0.7 multiply_add_fusion.4
  1.4 0.7 pad_maximum_fusion
  2.0 45.7 %all_gather.9 = f32[9,8192]{1,0:T(8,128)S(1)} all-gather(f32[9,512]{1,0:T(8,128)S(1)} %pad_maximum_fusion), channel_id=1, replica_groups=mesh['row'=16,'col'=2] {'row'}, dimensions={1}, use_global_device_ids=true | all-gather | bytes 313344 | tf_op jit(solution)/shard_map/all_gather | solution.py:62
  47.8 37.0 %all_gather.10 = f32[8,8192]{1,0:T(8,128)S(1)} all-gather(f32[8,512]{1,0:T(8,128)S(1)} %copy-done.1), channel_id=1, replica_groups=mesh['row'=16,'col'=2] {'row'}, dimensions={1}, use_global_device_ids=true | all-gather | bytes 278528 | tf_op jit(solution)/shard_map/all_gather | solution.py:50
  84.9 18.8 %while.28 = (s32[]{:T(128)}, f32[9,512]{1,0:T(8,128)S(1)}, f32[9,4096]{1,0:T(8,128)S(1)}, f32[8,512]{1,0:T(8,128)S(1)}, f32[8,4096]{1,0:T(8,128)S(1)}, /*index=5...) while((s32[]{:T(128)}, f32[9,512]{1,0:T(8,128)S(1)}, ...), condition=%wide.region_3.0_spmd.clone, body=%wide.region_2.0_spmd.clone.sunk | while | flops 72360976 | bytes 264517 | solution.py:40
  84.9 0.1 constant_dynamic-slice_fusion.6
  85.1 4.5 %fusion.133 = f32[9,512]{1,0:T(8,128)S(1)} fusion(f32[1024]{0:T(1024)S(1)} %bitcast.104, f32[512]{0:T(512)S(1)} %bitcast.120, f32[1024]{0:T(1024)S(1)} %bitcast.98, f32[512]{0:T(512)S(1)} %bitcast.121, f32[1024]{0:T(1024)S(1)} %bitcast.99, f32[512]{0:T(512)S(1)} %bitcast.122, f32[1024]{0:T(1024)S(1)} %bitcast.100, f32[512]{0:T(512)S(1)} %bitcast.123, ...), kind=kOutput, calls=%fused_computation.33.clone.1 | convolution fusion | flops 72360960 | bytes 165893 | tf_op jit(solution)/shard_map/while/body/eval_jaxpr/dot_general | solution.py:31
  89.6 0.1 constant_dynamic-slice_fusion.6
  89.8 4.5 %fusion.133 = f32[9,512]{1,0:T(8,128)S(1)} fusion(f32[1024]{0:T(1024)S(1)} %bitcast.104, f32[512]{0:T(512)S(1)} %bitcast.120, f32[1024]{0:T(1024)S(1)} %bitcast.98, f32[512]{0:T(512)S(1)} %bitcast.121, f32[1024]{0:T(1024)S(1)} %bitcast.99, f32[512]{0:T(512)S(1)} %bitcast.122, f32[1024]{0:T(1024)S(1)} %bitcast.100, f32[512]{0:T(512)S(1)} %bitcast.123, ...), kind=kOutput, calls=%fused_computation.33.clone.1 | convolution fusion | flops 72360960 | bytes 165893 | tf_op jit(solution)/shard_map/while/body/eval_jaxpr/dot_general | solution.py:31
  94.3 0.1 constant_dynamic-slice_fusion.6
  94.5 4.5 %fusion.133 = f32[9,512]{1,0:T(8,128)S(1)} fusion(f32[1024]{0:T(1024)S(1)} %bitcast.104, f32[512]{0:T(512)S(1)} %bitcast.120, f32[1024]{0:T(1024)S(1)} %bitcast.98, f32[512]{0:T(512)S(1)} %bitcast.121, f32[1024]{0:T(1024)S(1)} %bitcast.99, f32[512]{0:T(512)S(1)} %bitcast.122, f32[1024]{0:T(1024)S(1)} %bitcast.100, f32[512]{0:T(512)S(1)} %bitcast.123, ...), kind=kOutput, calls=%fused_computation.33.clone.1 | convolution fusion | flops 72360960 | bytes 165893 | tf_op jit(solution)/shard_map/while/body/eval_jaxpr/dot_general | solution.py:31
  99.0 0.1 constant_dynamic-slice_fusion.6
  99.2 4.5 %fusion.133 = f32[9,512]{1,0:T(8,128)S(1)} fusion(f32[1024]{0:T(1024)S(1)} %bitcast.104, f32[512]{0:T(512)S(1)} %bitcast.120, f32[1024]{0:T(1024)S(1)} %bitcast.98, f32[512]{0:T(512)S(1)} %bitcast.121, f32[1024]{0:T(1024)S(1)} %bitcast.99, f32[512]{0:T(512)S(1)} %bitcast.122, f32[1024]{0:T(1024)S(1)} %bitcast.100, f32[512]{0:T(512)S(1)} %bitcast.123, ...), kind=kOutput, calls=%fused_computation.33.clone.1 | convolution fusion | flops 72360960 | bytes 165893 | tf_op jit(solution)/shard_map/while/body/eval_jaxpr/dot_general | solution.py:31
  103.7 3.4 %psum.43 = f32[9,512]{1,0:T(8,128)S(1)} all-reduce(f32[9,512]{1,0:T(8,128)S(1)} %get-tuple-element.190), channel_id=1, replica_groups=mesh['row'=16,'col'=2] {'col'}, use_global_device_ids=true, to_apply=%region_4.0 | all-reduce | flops 4608 | bytes 36864 | tf_op jit(solution)/shard_map/psum | solution.py:65
  107.1 0.1 multiply_reduce_fusion.2
  107.3 38.5 %all-reduce = (f32[9]{0:T(128)S(1)}, f32[9]{0:T(128)S(1)}) all-reduce(f32[9]{0:T(128)S(1)} %get-tuple-element.229, f32[9]{0:T(128)S(1)} %get-tuple-element.228), channel_id=1, replica_groups=mesh['row'=16,'col'=2] {'row'}, use_global_device_ids=true, to_apply=%region_1.0 | all-reduce | flops 18 | bytes 144 | tf_op jit(solution)/shard_map/psum | solution.py:44
  145.7 0.2 multiply_reduce_fusion.1
  145.9 36.7 %psum.45 = f32[9]{0:T(128)S(1)} all-reduce(f32[9]{0:T(128)S(1)} %multiply_reduce_fusion.1), channel_id=1, replica_groups=mesh['row'=16,'col'=2] {'row'}, use_global_device_ids=true, to_apply=%region_8.0 | all-reduce | flops 9 | bytes 72 | tf_op jit(solution)/shard_map/psum | solution.py:44
  182.7 40.5 %all_gather.11 = f32[9,8192]{1,0:T(8,128)S(1)} all-gather(f32[9,512]{1,0:T(8,128)S(1)} %multiply_add_fusion.2), channel_id=1, replica_groups=mesh['row'=16,'col'=2] {'row'}, dimensions={1}, use_global_device_ids=true | all-gather | bytes 313344 | tf_op jit(solution)/shard_map/all_gather | solution.py:62
  223.3 18.8 %while.29 = (s32[]{:T(128)}, f32[9,512]{1,0:T(8,128)S(1)}, f32[9,4096]{1,0:T(8,128)S(1)}, f32[8,512]{1,0:T(8,128)S(1)}, f32[8,4096]{1,0:T(8,128)S(1)}, /*index=5...) while((s32[]{:T(128)}, f32[9,512]{1,0:T(8,128)S(1)}, ...), condition=%wide.region_10.0_spmd.clone, body=%wide.region_9.0_spmd.clone.sunk | while | flops 72360976 | bytes 264517 | solution.py:40
  223.3 0.2 constant_dynamic-slice_fusion.7
  223.5 4.5 %fusion.137 = f32[9,512]{1,0:T(8,128)S(1)} fusion(f32[1024]{0:T(1024)S(1)} %bitcast.112, f32[512]{0:T(512)S(1)} %bitcast.128, f32[1024]{0:T(1024)S(1)} %bitcast.106, f32[512]{0:T(512)S(1)} %bitcast.129, f32[1024]{0:T(1024)S(1)} %bitcast.107, f32[512]{0:T(512)S(1)} %bitcast.130, f32[1024]{0:T(1024)S(1)} %bitcast.108, f32[512]{0:T(512)S(1)} %bitcast.131, ...), kind=kOutput, calls=%fused_computation.92.clone.1 | convolution fusion | flops 72360960 | bytes 165893 | tf_op jit(solution)/shard_map/while/body/eval_jaxpr/dot_general | solution.py:31
  228.0 0.2 constant_dynamic-slice_fusion.7
  228.2 4.5 %fusion.137 = f32[9,512]{1,0:T(8,128)S(1)} fusion(f32[1024]{0:T(1024)S(1)} %bitcast.112, f32[512]{0:T(512)S(1)} %bitcast.128, f32[1024]{0:T(1024)S(1)} %bitcast.106, f32[512]{0:T(512)S(1)} %bitcast.129, f32[1024]{0:T(1024)S(1)} %bitcast.107, f32[512]{0:T(512)S(1)} %bitcast.130, f32[1024]{0:T(1024)S(1)} %bitcast.108, f32[512]{0:T(512)S(1)} %bitcast.131, ...), kind=kOutput, calls=%fused_computation.92.clone.1 | convolution fusion | flops 72360960 | bytes 165893 | tf_op jit(solution)/shard_map/while/body/eval_jaxpr/dot_general | solution.py:31
  232.7 0.2 constant_dynamic-slice_fusion.7
  232.9 4.5 %fusion.137 = f32[9,512]{1,0:T(8,128)S(1)} fusion(f32[1024]{0:T(1024)S(1)} %bitcast.112, f32[512]{0:T(512)S(1)} %bitcast.128, f32[1024]{0:T(1024)S(1)} %bitcast.106, f32[512]{0:T(512)S(1)} %bitcast.129, f32[1024]{0:T(1024)S(1)} %bitcast.107, f32[512]{0:T(512)S(1)} %bitcast.130, f32[1024]{0:T(1024)S(1)} %bitcast.108, f32[512]{0:T(512)S(1)} %bitcast.131, ...), kind=kOutput, calls=%fused_computation.92.clone.1 | convolution fusion | flops 72360960 | bytes 165893 | tf_op jit(solution)/shard_map/while/body/eval_jaxpr/dot_general | solution.py:31
  237.4 0.2 constant_dynamic-slice_fusion.7
  237.6 4.5 %fusion.137 = f32[9,512]{1,0:T(8,128)S(1)} fusion(f32[1024]{0:T(1024)S(1)} %bitcast.112, f32[512]{0:T(512)S(1)} %bitcast.128, f32[1024]{0:T(1024)S(1)} %bitcast.106, f32[512]{0:T(512)S(1)} %bitcast.129, f32[1024]{0:T(1024)S(1)} %bitcast.107, f32[512]{0:T(512)S(1)} %bitcast.130, f32[1024]{0:T(1024)S(1)} %bitcast.108, f32[512]{0:T(512)S(1)} %bitcast.131, ...), kind=kOutput, calls=%fused_computation.92.clone.1 | convolution fusion | flops 72360960 | bytes 165893 | tf_op jit(solution)/shard_map/while/body/eval_jaxpr/dot_general | solution.py:31
  242.1 3.4 %psum.46 = f32[9,512]{1,0:T(8,128)S(1)} all-reduce(f32[9,512]{1,0:T(8,128)S(1)} %get-tuple-element.191), channel_id=1, replica_groups=mesh['row'=16,'col'=2] {'col'}, use_global_device_ids=true, to_apply=%region_11.0 | all-reduce | flops 4608 | bytes 36864 | tf_op jit(solution)/shard_map/psum | solution.py:65
  245.5 0.2 multiply_reduce_fusion
  245.7 36.6 %psum.47 = f32[9]{0:T(128)S(1)} all-reduce(f32[9]{0:T(128)S(1)} %multiply_reduce_fusion), channel_id=1, replica_groups=mesh['row'=16,'col'=2] {'row'}, use_global_device_ids=true, to_apply=%region_13.0 | all-reduce | flops 9 | bytes 72 | tf_op jit(solution)/shard_map/psum | solution.py:66
  282.3 0.7 multiply_subtract_fusion
  (27 shorter events, 0.4 us)
Async XLA Ops:
  2.0 45.7 %copy-start.3 = (f32[8]{0:T(128)S(1)}, f32[8]{0:T(128)}, u32[]{:S(2)}) copy-start(f32[8]{0:T(128)} %param.10) | copy-start | bytes 100
  2.0 45.7 %copy-start.1 = (f32[8,512]{1,0:T(8,128)S(1)}, f32[8,512]{1,0:T(8,128)}, u32[]{:S(2)}) copy-start(f32[8,512]{1,0:T(8,128)} %param.9) | copy-start | bytes 49156
  84.9 22.2 %copy-start = (f32[512]{0:T(512)S(1)}, f32[512]{0:T(512)}, u32[]{:S(2)}) copy-start(f32[512]{0:T(512)} %param.12) | copy-start | bytes 6148
  84.9 22.2 %copy-start.2 = (f32[512]{0:T(512)S(1)}, f32[512]{0:T(512)}, u32[]{:S(2)}) copy-start(f32[512]{0:T(512)} %param.11) | copy-start | bytes 6148
where the time goes:
time: 283 us
  blocking collectives  242 us (86%)
  matrix products  36 us (13%)
  other arithmetic  2.89 us (1%)
    all_gather x2, blocking collectives, per_device(): whole_dirs = lax.all_gather(direction, 'row', axis=1, tiled=True)  86.2 us
    psum x2, blocking collectives, row_squares(): return lax.psum(jnp.sum(residual * residual, axis=1), 'row')  75.2 us
    all_gather x1, blocking collectives, per_device(): lax.all_gather(points, 'row', axis=1, tiled=True) * inverse_scale[:, None]  37 us
    psum x1, blocking collectives, per_device(): curve = lax.psum(jnp.sum(direction * image, axis=1), 'row')  36.6 us
    dot_general x8, matrix products, block_step(): lax.dot_general(dirs_here, kernel_tile, (((1,), (1,)), ((), ())), precisi...  36 us
    psum x2, blocking collectives, per_device(): image = lax.psum(partial_image, 'col') + noise[None, :] * direction  6.81 us

commit v1 on v0

v1 whole, which is shorter than its diff:
```python
import functools

import jax
import jax.numpy as jnp
from jax import lax
from jax.experimental import pallas as pl
from jax.experimental.pallas import tpu as pltpu
from jax.sharding import PartitionSpec as P

MESH = pl.DeviceIdType.MESH
LANES = 128
root_five = 5.0**0.5


def split(x):
    high = x.astype(jnp.bfloat16).astype(jnp.float32)
    rest = x - high
    mid = rest.astype(jnp.bfloat16).astype(jnp.float32)
    return high, mid, rest - mid


def augment(points, own):
    high, mid, low = split(points)
    norms = split(jnp.sum(points * points, axis=0, keepdims=True))
    rows = lax.broadcasted_iota(jnp.int32, points.shape, 0)
    first = 3 if own else 0
    ends = jnp.where(rows < 6, 1.0, 0.0)
    for place in range(3):
        ends = jnp.where(rows == first + place, norms[place], ends)
    if own:
        high, mid, low = -2.0 * high, -2.0 * mid, -2.0 * low
        parts = [high, mid, high, low, high, mid]
    else:
        parts = [high, high, mid, high, low, mid]
    return jnp.concatenate(parts + [ends, jnp.zeros_like(ends)], axis=0)


def sixteen(probes, tile):
    n = probes.shape[1]
    line = jnp.concatenate([tile[k : k + 1, :] for k in range(n // LANES)], axis=1)
    rows = lax.broadcasted_iota(jnp.int32, probes.shape, 0)
    return jnp.concatenate([probes, jnp.where(rows == 0, line, 0.0)], axis=0)


def halves(x):
    high = x.astype(jnp.bfloat16)
    mid = (x - high.astype(jnp.float32)).astype(jnp.bfloat16)
    return jnp.concatenate([high, mid], axis=0)


def scalars(values):
    lanes = lax.broadcasted_iota(jnp.int32, (8, LANES), 1)
    tile = jnp.zeros((8, LANES), jnp.float32)
    for k, value in enumerate(values):
        tile = jnp.where(lanes == k, value[0:8], tile)
        tile = jnp.where(lanes == len(values) + k, value[8:9], tile)
    return tile


def kernel(R, C, scale, points, noise, target, bits, sol, res,
           msg, slots_a, parts, vec, slots_b, scal_b, own_c, scal_c, k_hi, k_lo,
           send_a, recv_a, send_p, recv_p, send_b, recv_b, send_s, recv_s, send_c, recv_c):
    n = points.shape[1]
    G = R // C
    T = R // C
    sub = min(256, n)
    me_r = lax.axis_index("row")
    me_c = lax.axis_index("col")
    group = me_r // G
    spot = lax.rem(me_r, G)
    side = lax.rem(me_r, C)
    in_group = group == me_c

    barrier = pltpu.get_barrier_semaphore()

    def greet(k, carry):
        pl.semaphore_signal(barrier, inc=1, device_id=(lax.rem(me_r + k, R), side), device_id_type=MESH)
        return carry

    lax.fori_loop(1, R, greet, 0)
    for k in range(1, C):
        pl.semaphore_signal(barrier, inc=1, device_id=(me_r, lax.rem(me_c + k, C)), device_id_type=MESH)

    rows8 = lax.broadcasted_iota(jnp.int32, (8, 1), 0)
    lengths = jnp.full((8, 1), scale[0], jnp.float32)
    for f in range(1, 8):
        lengths = jnp.where(rows8 == f, scale[f], lengths)
    own_points = points[...] * (root_five / lengths)
    signs = 2.0 * bits[...].astype(jnp.float32) - 1.0
    own_target = target[...]
    msg[:, 0:n] = own_points
    msg[:, n : 2 * n] = signs
    msg[:, 2 * n :] = jnp.zeros((8, LANES), jnp.float32)
    for k in range(n // LANES):
        msg[k : k + 1, 2 * n :] = own_target[:, k * LANES : (k + 1) * LANES]

    pl.semaphore_wait(barrier, (T - jnp.where(side == me_c, 1, 0)) * C + C - 1)

    def target_row(k):
        return C * lax.rem(me_r // C + k, T) + me_c

    def copy_a(k):
        return pltpu.make_async_remote_copy(
            src_ref=msg, dst_ref=slots_a.at[spot], send_sem=send_a.at[k], recv_sem=recv_a.at[spot],
            device_id=(target_row(k), group), device_id_type=MESH)

    def copy_p(phase, k):
        return pltpu.make_async_remote_copy(
            src_ref=parts.at[phase, me_c], dst_ref=parts.at[phase, me_c],
            send_sem=send_p.at[phase, k - 1], recv_sem=recv_p.at[phase, me_c],
            device_id=(me_r, lax.rem(me_c + k, C)), device_id_type=MESH)

    def copy_b(k):
        return pltpu.make_async_remote_copy(
            src_ref=vec, dst_ref=slots_b.at[spot], send_sem=send_b.at[k], recv_sem=recv_b.at[spot],
            device_id=(target_row(k), group), device_id_type=MESH)

    def copy_s(k, g):
        return pltpu.make_async_remote_copy(
            src_ref=scal_b.at[me_r], dst_ref=scal_b.at[me_r], send_sem=send_s.at[g - 1, k], recv_sem=recv_s.at[me_r],
            device_id=(target_row(k), lax.rem(group + g, C)), device_id_type=MESH)

    def copy_c(k, g):
        return pltpu.make_async_remote_copy(
            src_ref=own_c, dst_ref=scal_c.at[me_r], send_sem=send_c.at[g, k], recv_sem=recv_c.at[me_r],
            device_id=(target_row(k), g), device_id_type=MESH)

    def over_targets(action):
        def one(k, carry):
            @pl.when(target_row(k) != me_r)
            def _():
                action(k)
            return carry
        lax.fori_loop(0, T, one, 0)

    over_targets(lambda k: copy_a(k).start())

    @pl.when(in_group)
    def _():
        slots_a[spot] = msg[...]

    own_aug = augment(own_points, True).astype(jnp.bfloat16)

    def wait_slot(buffer, sem, t, like):
        pltpu.make_async_remote_copy(
            src_ref=like, dst_ref=buffer.at[t], send_sem=send_a.at[0], recv_sem=sem.at[t],
            device_id=(me_r, me_c), device_id_type=MESH).wait_recv()

    def build(k, accum):
        t = lax.rem(spot + k, G)

        @pl.when(me_c * G + t != me_r)
        def _():
            wait_slot(slots_a, recv_a, t, msg)

        columns = augment(slots_a[t, :, 0:n], False).T.astype(jnp.bfloat16)
        dirs = halves(sixteen(slots_a[t, :, n : 2 * n], slots_a[t, :, 2 * n :]))
        for j in range(0, n, sub):
            s2 = jnp.dot(columns[j : j + sub, :], own_aug, preferred_element_type=jnp.float32)
            s2 = jnp.maximum(s2, 1e-12)
            s = s2 * lax.rsqrt(s2)
            value = (s2 * (1.0 / 3.0) + s + 1.0) * jnp.exp(-s)
            high = value.astype(jnp.bfloat16)
            low = (value - high.astype(jnp.float32)).astype(jnp.bfloat16)
            k_hi[t, j : j + sub, :] = high
            k_lo[t, j : j + sub, :] = low
            here = dirs[:, j : j + sub]
            accum = accum + jnp.dot(here, high, preferred_element_type=jnp.float32)
            accum = accum + jnp.dot(here, low, preferred_element_type=jnp.float32)
        return accum

    zero = jnp.zeros((32, n), jnp.float32)
    accum = lax.fori_loop(0, G, build, zero)

    def across(phase, accum):
        parts[phase, me_c] = accum[0:16] + accum[16:32]
        for k in range(1, C):
            copy_p(phase, k).start()
        for k in range(1, C):
            c = lax.rem(me_c + k, C)
            pltpu.make_async_remote_copy(
                src_ref=parts.at[phase, me_c], dst_ref=parts.at[phase, c], send_sem=send_p.at[phase, 0],
                recv_sem=recv_p.at[phase, c], device_id=(me_r, me_c), device_id_type=MESH).wait_recv()
        total = parts[phase, 0]
        for c in range(1, C):
            total = total + parts[phase, c]
        return total

    noise_row = noise[...]
    start = sixteen(signs, msg[:, 2 * n :])
    image = across(0, accum) + noise_row * start

    def dot(a, b):
        return jnp.sum(a * b, axis=1, keepdims=True)

    own_scal = scalars([dot(start, image), dot(image, image), dot(start, start)])
    vec[:, 0:n] = image[0:8]
    vec[:, n : n + LANES] = jnp.zeros((8, LANES), jnp.float32)
    for k in range(n // LANES):
        vec[k : k + 1, n : n + LANES] = image[8:9, k * LANES : (k + 1) * LANES]
    vec[:, n + LANES :] = own_scal
    scal_b[me_r] = own_scal

    def send_image(k):
        copy_b(k).start()
        for g in range(1, C):
            copy_s(k, g).start()

    over_targets(send_image)

    @pl.when(in_group)
    def _():
        slots_b[spot] = vec[...]

    def receive_image(b, carry):
        @pl.when(b != me_r)
        def _():
            @pl.when(b // G == me_c)
            def _():
                t = lax.rem(b, G)
                wait_slot(slots_b, recv_b, t, vec)
                scal_b[b] = slots_b[t, :, n + LANES :]

            @pl.when(b // G != me_c)
            def _():
                wait_slot(scal_b, recv_s, b, own_c)
        return carry

    lax.fori_loop(0, R, receive_image, 0)
    total = jnp.sum(scal_b[...], axis=0)

    def pick(tile, k, count):
        return jnp.concatenate([tile[:, k : k + 1], tile[:, count + k : count + k + 1]], axis=0)

    curve, square, norm = pick(total, 0, 3), pick(total, 1, 3), pick(total, 2, 3)
    alpha = norm / curve
    norm_next = alpha * alpha * square - norm
    beta = norm_next / norm

    def again(t, accum):
        first = sixteen(slots_a[t, :, n : 2 * n], slots_a[t, :, 2 * n :])
        moved = sixteen(slots_b[t, :, 0:n], slots_b[t, :, n : n + LANES])
        dirs = halves((first - alpha * moved) + beta * first)
        accum = accum + jnp.dot(dirs, k_hi[t], preferred_element_type=jnp.float32)
        return accum + jnp.dot(dirs, k_lo[t], preferred_element_type=jnp.float32)

    accum = lax.fori_loop(0, G, again, zero)
    residual = start - alpha * image
    direction = residual + beta * start
    image = across(1, accum) + noise_row * direction
    own_scal = scalars([dot(direction, image)])
    own_c[...] = own_scal
    scal_c[me_r] = own_scal

    def send_curve(k):
        for g in range(C):
            copy_c(k, g).start()

    over_targets(send_curve)

    def receive_curve(b, carry):
        @pl.when(b != me_r)
        def _():
            wait_slot(scal_c, recv_c, b, own_c)
        return carry

    lax.fori_loop(0, R, receive_curve, 0)
    alpha_last = norm_next / pick(jnp.sum(scal_c[...], axis=0), 0, 1)
    answer = alpha * start + alpha_last * direction
    residual = residual - alpha_last * image
    sol[0:8, :] = answer[0:8]
    sol[8:9, :] = answer[8:9]
    res[0:8, :] = residual[0:8]
    res[8:9, :] = residual[8:9]

    def finish(k):
        copy_a(k).wait_send()
        copy_b(k).wait_send()
        for g in range(1, C):
            copy_s(k, g).wait_send()
        for g in range(C):
            copy_c(k, g).wait_send()

    over_targets(finish)
    for phase in range(2):
        for k in range(1, C):
            copy_p(phase, k).wait_send()


def per_device(R, C, points, lengthscale, noise, target, probe_bits):
    n = points.shape[1]
    G = T = R // C
    f32, bf16, dma = jnp.float32, jnp.bfloat16, pltpu.SemaphoreType.DMA
    vmem = pl.BlockSpec(memory_space=pltpu.VMEM)
    return pl.pallas_call(
        functools.partial(kernel, R, C),
        out_shape=(jax.ShapeDtypeStruct((9, n), f32),) * 2,
        in_specs=[pl.BlockSpec(memory_space=pltpu.SMEM)] + [vmem] * 4,
        out_specs=(vmem, vmem),
        scratch_shapes=[
            pltpu.VMEM((8, 2 * n + LANES), f32),
            pltpu.VMEM((G, 8, 2 * n + LANES), f32),
            pltpu.VMEM((2, C, 16, n), f32),
            pltpu.VMEM((8, n + 2 * LANES), f32),
            pltpu.VMEM((G, 8, n + 2 * LANES), f32),
            pltpu.VMEM((R, 8, LANES), f32),
            pltpu.VMEM((8, LANES), f32),
            pltpu.VMEM((R, 8, LANES), f32),
            pltpu.VMEM((G, n, n), bf16),
            pltpu.VMEM((G, n, n), bf16),
            dma((T,)), dma((G,)), dma((2, C - 1)), dma((2, C)), dma((T,)), dma((G,)),
            dma((C - 1, T)), dma((R,)), dma((C, T)), dma((R,)),
        ],
        compiler_params=pltpu.CompilerParams(
            collective_id=0, has_side_effects=True, vmem_limit_bytes=40 * 1024 * 1024
        ),
    )(lengthscale, points, noise.reshape(1, n), target.reshape(1, n), probe_bits)


def solution(mesh):
    return jax.shard_map(
        functools.partial(per_device, mesh.shape["row"], mesh.shape["col"]),
        mesh=mesh,
        in_specs=(P(None, "row"), P(), P("row"), P("row"), P(None, "row")),
        out_specs=(P(None, "row"), P(None, "row")),
        check_vma=False,
    )
```

time: 283 us -> 44 us (0.16)
  blocking collectives: 242 us -> 0 us
  Pallas kernels: 0 us -> 39 us
  matrix products: 36 us -> 0 us
  other arithmetic: 2.89 us -> 0 us
    all_gather x3 -> x0, blocking collectives: 123 us -> none  [the longest x2 86.2 us: per_device(): whole_dirs = lax.all_gather(direction, 'row', axis=1, tiled=True)]
    psum x5 -> x0, blocking collectives: 119 us -> none  [the longest x2 75.2 us: row_squares(): return lax.psum(jnp.sum(residual * residual, axis=1), 'row')]
    pallas_call x0 -> x1, Pallas kernels: none -> 39 us  [per_device(): pl.pallas_call(functools.partial(kernel, R, C), out_shape=(jax.ShapeDtype...]
    dot_general x8 -> x0, matrix products: 36 us -> none  [block_step(): lax.dot_general(dirs_here, kernel_tile, (((1,), (1,)), ((), ())), precisi...]
    unnamed x8 -> x12, local copies, waits for them, and re-layouts: 0.01 us -> 4.02 us
where the time goes in v1:
time: 44 us; the launch traced here: 43.7 us
  Pallas kernels  39 us (89%)
  local copies, waits for them, and re-layouts  4.02 us (9%)
  between operations  0.66 us (2%)
    pallas_call x1, Pallas kernels, per_device(): pl.pallas_call(functools.partial(kernel, R, C), out_shape=(jax.ShapeDtype...  39 us
    unnamed x12, local copies, waits for them, and re-layouts  4.02 us

profile of v1, /device:TPU:0, one launch (start us, length us, event | category | flops | bytes accessed | tf_op | source)
XLA Modules:
  0.0 43.7 jit_solution(10202839659301494970)
XLA Ops:
  0.6 0.0 copy-start.2
  0.6 0.0 copy-start.4
  0.7 0.7 %copy-done.2 = f32[512]{0:T(512)S(1)} copy-done((f32[512]{0:T(512)S(1)}, f32[512]{0:T(512)}, u32[]{:S(2)}) %copy-start.2) | copy-done | bytes 2072
  1.3 0.0 copy-done.4
  1.3 0.0 copy-start
  1.3 0.7 %copy-done = f32[8,512]{1,0:T(8,128)S(1)} copy-done((f32[8,512]{1,0:T(8,128)S(1)}, f32[8,512]{1,0:T(8,128)}, u32[]{:S(2)}) %copy-start) | copy-done | bytes 16408
  2.0 0.0 copy-start.1
  2.0 0.7 %copy-done.1 = s32[8,512]{1,0:T(8,128)S(1)} copy-done((s32[8,512]{1,0:T(8,128)S(1)}, s32[8,512]{1,0:T(8,128)}, u32[]{:S(2)}) %copy-start.1) | copy-done | bytes 16408
  2.8 0.0 copy-start.3
  2.8 0.7 %copy-done.3 = f32[512]{0:T(512)S(1)} copy-done((f32[512]{0:T(512)S(1)}, f32[512]{0:T(512)}, u32[]{:S(2)}) %copy-start.3) | copy-done | bytes 2072
  3.4 39.0 %shard_map.68 = (f32[9,512]{1,0:T(8,128)S(1)}, f32[9,512]{1,0:T(8,128)S(1)}) custom-call(f32[8]{0:T(128)S(1)} %copy-done.4, f32[8,512]{1,0:T(8,128)S(1)} %copy-done, f32[1,512]{1,0:T(1,128)S(1)} %bitcast.2, f32[1,512]{1,0:T(1,128)S(1)} %bitcast.3, s32[8,512]{1,0:T(8,128)S(1)} %copy-done.1), custom_call_target="tpu_custom_call" | custom-call | tf_op jit(solution)/shard_map/pallas_call | solution.py:295
  42.5 0.6 %copy.9 = f32[9,512]{1,0:T(8,128)} copy(f32[9,512]{1,0:T(8,128)S(1)} %get-tuple-element.4) | data formatting | bytes 36864
  43.1 0.6 %copy.10 = f32[9,512]{1,0:T(8,128)} copy(f32[9,512]{1,0:T(8,128)S(1)} %get-tuple-element.5) | data formatting | bytes 36864
Async XLA Ops:
  0.6 0.7 %copy-start.2 = (f32[512]{0:T(512)S(1)}, f32[512]{0:T(512)}, u32[]{:S(2)}) copy-start(f32[512]{0:T(512)} %param.7) | copy-start | bytes 6148
  0.6 0.7 %copy-start.4 = (f32[8]{0:T(128)S(1)}, f32[8]{0:T(128)}, u32[]{:S(2)}) copy-start(f32[8]{0:T(128)} %scale.1) | copy-start | bytes 100
  1.3 0.7 %copy-start = (f32[8,512]{1,0:T(8,128)S(1)}, f32[8,512]{1,0:T(8,128)}, u32[]{:S(2)}) copy-start(f32[8,512]{1,0:T(8,128)} %points.1) | copy-start | bytes 49156
  2.0 0.7 %copy-start.1 = (s32[8,512]{1,0:T(8,128)S(1)}, s32[8,512]{1,0:T(8,128)}, u32[]{:S(2)}) copy-start(s32[8,512]{1,0:T(8,128)} %bits.1) | copy-start | bytes 49156
  2.8 0.7 %copy-start.3 = (f32[512]{0:T(512)S(1)}, f32[512]{0:T(512)}, u32[]{:S(2)}) copy-start(f32[512]{0:T(512)} %param.8) | copy-start | bytes 6148

commit v2 on v1

--- a/solution.py
+++ b/solution.py
@@ -57,9 +57,9 @@
     return tile
 
 
-def kernel(R, C, scale, points, noise, target, bits, sol, res,
-           msg, slots_a, parts, vec, slots_b, scal_b, own_c, scal_c, k_hi, k_lo,
-           send_a, recv_a, send_p, recv_p, send_b, recv_b, send_s, recv_s, send_c, recv_c):
+def kernel(R, C, scale_in, points_in, noise_in, target_in, bits_in, sol, res,
+           scale, points, noise, target, bits, msg, slots_a, msg_v, slots_v, parts, vec, slots_b, scal_b, own_c, scal_c, k_hi, k_lo,
+           load, send_a, recv_a, send_v, recv_v, send_p, recv_p, send_b, recv_b, send_s, recv_s, send_c, recv_c):
     n = points.shape[1]
     G = R // C
     T = R // C
@@ -71,6 +71,14 @@
     side = lax.rem(me_r, C)
     in_group = group == me_c
 
+    loads = [
+        pltpu.make_async_copy(source, here, load.at[k])
+        for k, (source, here) in enumerate(
+            [(scale_in, scale), (points_in, points), (bits_in, bits), (target_in, target), (noise_in, noise)])
+    ]
+    for one in loads:
+        one.start()
+
     barrier = pltpu.get_barrier_semaphore()
 
     def greet(k, carry):
@@ -80,6 +88,9 @@
     lax.fori_loop(1, R, greet, 0)
     for k in range(1, C):
         pl.semaphore_signal(barrier, inc=1, device_id=(me_r, lax.rem(me_c + k, C)), device_id_type=MESH)
+
+    for one in loads:
+        one.wait()
 
     rows8 = lax.broadcasted_iota(jnp.int32, (8, 1), 0)
     lengths = jnp.full((8, 1), scale[0], jnp.float32)
@@ -88,11 +99,11 @@
     own_points = points[...] * (root_five / lengths)
     signs = 2.0 * bits[...].astype(jnp.float32) - 1.0
     own_target = target[...]
-    msg[:, 0:n] = own_points
-    msg[:, n : 2 * n] = signs
-    msg[:, 2 * n :] = jnp.zeros((8, LANES), jnp.float32)
+    msg[...] = own_points
+    msg_v[:, 0:n] = signs
+    msg_v[:, n:] = jnp.zeros((8, LANES), jnp.float32)
     for k in range(n // LANES):
-        msg[k : k + 1, 2 * n :] = own_target[:, k * LANES : (k + 1) * LANES]
+        msg_v[k : k + 1, n:] = own_target[:, k * LANES : (k + 1) * LANES]
 
     pl.semaphore_wait(barrier, (T - jnp.where(side == me_c, 1, 0)) * C + C - 1)
 
@@ -102,6 +113,11 @@
     def copy_a(k):
         return pltpu.make_async_remote_copy(
             src_ref=msg, dst_ref=slots_a.at[spot], send_sem=send_a.at[k], recv_sem=recv_a.at[spot],
+            device_id=(target_row(k), group), device_id_type=MESH)
+
+    def copy_v(k):
+        return pltpu.make_async_remote_copy(
+            src_ref=msg_v, dst_ref=slots_v.at[spot], send_sem=send_v.at[k], recv_sem=recv_v.at[spot],
             device_id=(target_row(k), group), device_id_type=MESH)
 
     def copy_p(phase, k):
@@ -133,11 +149,12 @@
             return carry
         lax.fori_loop(0, T, one, 0)
 
-    over_targets(lambda k: copy_a(k).start())
+    over_targets(lambda k: (copy_a(k).start(), copy_v(k).start()))
 
     @pl.when(in_group)
     def _():
         slots_a[spot] = msg[...]
+        slots_v[spot] = msg_v[...]
 
     own_aug = augment(own_points, True).astype(jnp.bfloat16)
 
@@ -146,31 +163,47 @@
             src_ref=like, dst_ref=buffer.at[t], send_sem=send_a.at[0], recv_sem=sem.at[t],
             device_id=(me_r, me_c), device_id_type=MESH).wait_recv()
 
-    def build(k, accum):
-        t = lax.rem(spot + k, G)
-
+    first_spot = jnp.where(in_group, spot, G - 1)
+
+    def at(k):
+        return lax.rem(first_spot - k + G, G)
+
+    def arrive(buffer, sem, t, like):
         @pl.when(me_c * G + t != me_r)
         def _():
-            wait_slot(slots_a, recv_a, t, msg)
-
-        columns = augment(slots_a[t, :, 0:n], False).T.astype(jnp.bfloat16)
-        dirs = halves(sixteen(slots_a[t, :, n : 2 * n], slots_a[t, :, 2 * n :]))
+            wait_slot(buffer, sem, t, like)
+
+    def build(t):
+        columns = augment(slots_a[t], False).T.astype(jnp.bfloat16)
         for j in range(0, n, sub):
             s2 = jnp.dot(columns[j : j + sub, :], own_aug, preferred_element_type=jnp.float32)
             s2 = jnp.maximum(s2, 1e-12)
             s = s2 * lax.rsqrt(s2)
             value = (s2 * (1.0 / 3.0) + s + 1.0) * jnp.exp(-s)
-            high = value.astype(jnp.bfloat16)
-            low = (value - high.astype(jnp.float32)).astype(jnp.bfloat16)
-            k_hi[t, j : j + sub, :] = high
-            k_lo[t, j : j + sub, :] = low
-            here = dirs[:, j : j + sub]
-            accum = accum + jnp.dot(here, high, preferred_element_type=jnp.float32)
-            accum = accum + jnp.dot(here, low, preferred_element_type=jnp.float32)
+            top = value.astype(jnp.bfloat16)
+            k_hi[t, j : j + sub, :] = top
+            k_lo[t, j : j + sub, :] = (value - top.astype(jnp.float32)).astype(jnp.bfloat16)
+
+    def multiply(t, dirs, accum):
+        accum = accum + jnp.dot(dirs, k_hi[t], preferred_element_type=jnp.float32)
+        return accum + jnp.dot(dirs, k_lo[t], preferred_element_type=jnp.float32)
+
+    def first_of(t):
+        return sixteen(slots_v[t, :, 0:n], slots_v[t, :, n:])
+
+    def step(k, accum):
+        arrive(slots_a, recv_a, at(k), msg)
+        arrive(slots_v, recv_v, at(k - 1), msg_v)
+        accum = multiply(at(k - 1), halves(first_of(at(k - 1))), accum)
+        build(at(k))
         return accum
 
     zero = jnp.zeros((32, n), jnp.float32)
-    accum = lax.fori_loop(0, G, build, zero)
+    arrive(slots_a, recv_a, at(0), msg)
+    build(at(0))
+    accum = lax.fori_loop(1, G, step, zero)
+    arrive(slots_v, recv_v, at(G - 1), msg_v)
+    accum = multiply(at(G - 1), halves(first_of(at(G - 1))), accum)
 
     def across(phase, accum):
         parts[phase, me_c] = accum[0:16] + accum[16:32]
@@ -187,7 +220,7 @@
         return total
 
     noise_row = noise[...]
-    start = sixteen(signs, msg[:, 2 * n :])
+    start = sixteen(signs, msg_v[:, n:])
     image = across(0, accum) + noise_row * start
 
     def dot(a, b):
@@ -238,11 +271,9 @@
     beta = norm_next / norm
 
     def again(t, accum):
-        first = sixteen(slots_a[t, :, n : 2 * n], slots_a[t, :, 2 * n :])
+        first = first_of(t)
         moved = sixteen(slots_b[t, :, 0:n], slots_b[t, :, n : n + LANES])
-        dirs = halves((first - alpha * moved) + beta * first)
-        accum = accum + jnp.dot(dirs, k_hi[t], preferred_element_type=jnp.float32)
-        return accum + jnp.dot(dirs, k_lo[t], preferred_element_type=jnp.float32)
+        return multiply(t, halves((first - alpha * moved) + beta * first), accum)
 
     accum = lax.fori_loop(0, G, again, zero)
     residual = start - alpha * image
@@ -275,6 +306,7 @@
 
     def finish(k):
         copy_a(k).wait_send()
+        copy_v(k).wait_send()
         copy_b(k).wait_send()
         for g in range(1, C):
             copy_s(k, g).wait_send()
@@ -295,11 +327,18 @@
     return pl.pallas_call(
         functools.partial(kernel, R, C),
         out_shape=(jax.ShapeDtypeStruct((9, n), f32),) * 2,
-        in_specs=[pl.BlockSpec(memory_space=pltpu.SMEM)] + [vmem] * 4,
+        in_specs=[pl.BlockSpec(memory_space=pl.ANY)] * 5,
         out_specs=(vmem, vmem),
         scratch_shapes=[
-            pltpu.VMEM((8, 2 * n + LANES), f32),
-            pltpu.VMEM((G, 8, 2 * n + LANES), f32),
+            pltpu.SMEM((8,), f32),
+            pltpu.VMEM((8, n), f32),
+            pltpu.VMEM((1, n), f32),
+            pltpu.VMEM((1, n), f32),
+            pltpu.VMEM((8, n), jnp.int32),
+            pltpu.VMEM((8, n), f32),
+            pltpu.VMEM((G, 8, n), f32),
+            pltpu.VMEM((8, n + LANES), f32),
+            pltpu.VMEM((G, 8, n + LANES), f32),
             pltpu.VMEM((2, C, 16, n), f32),
             pltpu.VMEM((8, n + 2 * LANES), f32),
             pltpu.VMEM((G, 8, n + 2 * LANES), f32),
@@ -308,11 +347,11 @@
             pltpu.VMEM((R, 8, LANES), f32),
             pltpu.VMEM((G, n, n), bf16),
             pltpu.VMEM((G, n, n), bf16),
-            dma((T,)), dma((G,)), dma((2, C - 1)), dma((2, C)), dma((T,)), dma((G,)),
+            dma((5,)), dma((T,)), dma((G,)), dma((T,)), dma((G,)), dma((2, C - 1)), dma((2, C)), dma((T,)), dma((G,)),
             dma((C - 1, T)), dma((R,)), dma((C, T)), dma((R,)),
         ],
         compiler_params=pltpu.CompilerParams(
-            collective_id=0, has_side_effects=True, vmem_limit_bytes=40 * 1024 * 1024
+            collective_id=0, has_side_effects=True, vmem_limit_bytes=60 * 1024 * 1024
         ),
     )(lengthscale, points, noise.reshape(1, n), target.reshape(1, n), probe_bits)
 

time: 44 us -> 40.5 us (0.920)
  local copies, waits for them, and re-layouts: 4.02 us -> 2 us
  Pallas kernels: 39 us -> 37.6 us
    unnamed x12 -> x4, local copies, waits for them, and re-layouts: 4.02 us -> 2 us
    pallas_call x1, Pallas kernels: 39 us -> 37.6 us  [per_device(): pl.pallas_call(functools.partial(kernel, R, C), out_shape=(jax.ShapeDtype...]
where the time goes in v2:
time: 40.5 us; the launch traced here: 40.3 us
  Pallas kernels  37.6 us (93%)
  local copies, waits for them, and re-layouts  2 us (5%)
  between operations  0.65 us (2%)
    pallas_call x1, Pallas kernels, per_device(): pl.pallas_call(functools.partial(kernel, R, C), out_shape=(jax.ShapeDtype...  37.6 us
    unnamed x4, local copies, waits for them, and re-layouts  2 us

profile of v2, /device:TPU:0, one launch (start us, length us, event | category | flops | bytes accessed | tf_op | source)
XLA Modules:
  0.0 40.3 jit_solution(10318144583958443250)
XLA Ops:
  0.6 37.6 %shard_map.68 = (f32[9,512]{1,0:T(8,128)}, f32[9,512]{1,0:T(8,128)}) custom-call(f32[8]{0:T(128)} %scale_in.1, f32[8,512]{1,0:T(8,128)} %points_in.1, f32[1,512]{1,0:T(1,128)} %bitcast.2, f32[1,512]{1,0:T(1,128)} %bitcast.3, s32[8,512]{1,0:T(8,128)} %bits_in.1), custom_call_target="tpu_custom_call" | custom-call | tf_op jit(solution)/shard_map/pallas_call | solution.py:327
  38.3 0.0 copy-start
  38.3 1.4 %copy.9 = f32[9,512]{1,0:T(8,128)} copy(f32[9,512]{1,0:T(8,128)} %get-tuple-element.4) | data formatting | bytes 36864
  39.7 0.0 copy-done
  39.7 0.6 %copy.10 = f32[9,512]{1,0:T(8,128)} copy(f32[9,512]{1,0:T(8,128)S(1)} %copy-done) | data formatting | bytes 36864
Async XLA Ops:
  38.3 1.4 %copy-start = (f32[9,512]{1,0:T(8,128)S(1)}, f32[9,512]{1,0:T(8,128)}, u32[]{:S(2)}) copy-start(f32[9,512]{1,0:T(8,128)} %get-tuple-element.5) | copy-start | bytes 55300

commit v3 on v2

--- a/solution.py
+++ b/solution.py
@@ -49,15 +49,21 @@
 
 
 def scalars(values):
-    lanes = lax.broadcasted_iota(jnp.int32, (8, LANES), 1)
-    tile = jnp.zeros((8, LANES), jnp.float32)
+    lanes = lax.broadcasted_iota(jnp.int32, (16, LANES), 1)
+    rows = lax.broadcasted_iota(jnp.int32, (16, LANES), 0)
+    spread = jnp.zeros((16, LANES), jnp.float32)
     for k, value in enumerate(values):
-        tile = jnp.where(lanes == k, value[0:8], tile)
-        tile = jnp.where(lanes == len(values) + k, value[8:9], tile)
-    return tile
-
-
-def kernel(R, C, scale_in, points_in, noise_in, target_in, bits_in, sol, res,
+        spread = jnp.where(lanes == rows + 16 * k, value, spread)
+    return jnp.sum(spread, axis=0, keepdims=True)
+
+
+def pick(line, k):
+    lanes = lax.broadcasted_iota(jnp.int32, (16, LANES), 1)
+    rows = lax.broadcasted_iota(jnp.int32, (16, LANES), 0)
+    return jnp.sum(jnp.where(lanes == rows + 16 * k, line, 0.0), axis=1, keepdims=True)
+
+
+def kernel(R, C, scale_in, points_in, noise_in, target_in, bits_in, both,
            scale, points, noise, target, bits, msg, slots_a, msg_v, slots_v, parts, vec, slots_b, scal_b, own_c, scal_c, k_hi, k_lo,
            load, send_a, recv_a, send_v, recv_v, send_p, recv_p, send_b, recv_b, send_s, recv_s, send_c, recv_c):
     n = points.shape[1]
@@ -228,10 +234,10 @@
 
     own_scal = scalars([dot(start, image), dot(image, image), dot(start, start)])
     vec[:, 0:n] = image[0:8]
-    vec[:, n : n + LANES] = jnp.zeros((8, LANES), jnp.float32)
+    vec[:, n:] = jnp.zeros((8, LANES), jnp.float32)
     for k in range(n // LANES):
-        vec[k : k + 1, n : n + LANES] = image[8:9, k * LANES : (k + 1) * LANES]
-    vec[:, n + LANES :] = own_scal
+        vec[k : k + 1, n:] = image[8:9, k * LANES : (k + 1) * LANES]
+    vec[7:8, n:] = own_scal
     scal_b[me_r] = own_scal
 
     def send_image(k):
@@ -252,7 +258,7 @@
             def _():
                 t = lax.rem(b, G)
                 wait_slot(slots_b, recv_b, t, vec)
-                scal_b[b] = slots_b[t, :, n + LANES :]
+                scal_b[b] = slots_b[t, 7:8, n:]
 
             @pl.when(b // G != me_c)
             def _():
@@ -262,20 +268,18 @@
     lax.fori_loop(0, R, receive_image, 0)
     total = jnp.sum(scal_b[...], axis=0)
 
-    def pick(tile, k, count):
-        return jnp.concatenate([tile[:, k : k + 1], tile[:, count + k : count + k + 1]], axis=0)
-
-    curve, square, norm = pick(total, 0, 3), pick(total, 1, 3), pick(total, 2, 3)
-    alpha = norm / curve
+    curve, square, norm = pick(total, 0), pick(total, 1), pick(total, 2)
+    real = lax.broadcasted_iota(jnp.int32, (16, 1), 0) < 9
+    alpha = jnp.where(real, norm / curve, 0.0)
     norm_next = alpha * alpha * square - norm
-    beta = norm_next / norm
+    beta = jnp.where(real, norm_next / norm, 0.0)
 
     def again(t, accum):
         first = first_of(t)
-        moved = sixteen(slots_b[t, :, 0:n], slots_b[t, :, n : n + LANES])
+        moved = sixteen(slots_b[t, :, 0:n], slots_b[t, :, n:])
         return multiply(t, halves((first - alpha * moved) + beta * first), accum)
 
-    accum = lax.fori_loop(0, G, again, zero)
+    accum = lax.fori_loop(0, G, again, zero, unroll=8)
     residual = start - alpha * image
     direction = residual + beta * start
     image = across(1, accum) + noise_row * direction
@@ -296,13 +300,11 @@
         return carry
 
     lax.fori_loop(0, R, receive_curve, 0)
-    alpha_last = norm_next / pick(jnp.sum(scal_c[...], axis=0), 0, 1)
+    alpha_last = norm_next / pick(jnp.sum(scal_c[...], axis=0), 0)
     answer = alpha * start + alpha_last * direction
     residual = residual - alpha_last * image
-    sol[0:8, :] = answer[0:8]
-    sol[8:9, :] = answer[8:9]
-    res[0:8, :] = residual[0:8]
-    res[8:9, :] = residual[8:9]
+    both[0] = answer
+    both[1] = residual
 
     def finish(k):
         copy_a(k).wait_send()
@@ -324,11 +326,11 @@
     G = T = R // C
     f32, bf16, dma = jnp.float32, jnp.bfloat16, pltpu.SemaphoreType.DMA
     vmem = pl.BlockSpec(memory_space=pltpu.VMEM)
-    return pl.pallas_call(
+    both = pl.pallas_call(
         functools.partial(kernel, R, C),
-        out_shape=(jax.ShapeDtypeStruct((9, n), f32),) * 2,
+        out_shape=jax.ShapeDtypeStruct((2, 16, n), f32),
         in_specs=[pl.BlockSpec(memory_space=pl.ANY)] * 5,
-        out_specs=(vmem, vmem),
+        out_specs=vmem,
         scratch_shapes=[
             pltpu.SMEM((8,), f32),
             pltpu.VMEM((8, n), f32),
@@ -340,11 +342,11 @@
             pltpu.VMEM((8, n + LANES), f32),
             pltpu.VMEM((G, 8, n + LANES), f32),
             pltpu.VMEM((2, C, 16, n), f32),
-            pltpu.VMEM((8, n + 2 * LANES), f32),
-            pltpu.VMEM((G, 8, n + 2 * LANES), f32),
-            pltpu.VMEM((R, 8, LANES), f32),
-            pltpu.VMEM((8, LANES), f32),
-            pltpu.VMEM((R, 8, LANES), f32),
+            pltpu.VMEM((8, n + LANES), f32),
+            pltpu.VMEM((G, 8, n + LANES), f32),
+            pltpu.VMEM((R, 1, LANES), f32),
+            pltpu.VMEM((1, LANES), f32),
+            pltpu.VMEM((R, 1, LANES), f32),
             pltpu.VMEM((G, n, n), bf16),
             pltpu.VMEM((G, n, n), bf16),
             dma((5,)), dma((T,)), dma((G,)), dma((T,)), dma((G,)), dma((2, C - 1)), dma((2, C)), dma((T,)), dma((G,)),
@@ -354,6 +356,7 @@
             collective_id=0, has_side_effects=True, vmem_limit_bytes=60 * 1024 * 1024
         ),
     )(lengthscale, points, noise.reshape(1, n), target.reshape(1, n), probe_bits)
+    return both[0, :9], both[1, :9]
 
 
 def solution(mesh):

time: 40.5 us -> 37.6 us (0.928)
  Pallas kernels: 37.6 us -> 35.3 us
  local copies, waits for them, and re-layouts: 2 us -> 1.41 us
    pallas_call x1, Pallas kernels: 37.6 us -> 35.3 us  [per_device(): pl.pallas_call(functools.partial(kernel, R, C), out_shape=jax.ShapeDtypeS...]
    unnamed x4 -> x0, local copies, waits for them, and re-layouts: 2 us -> none
    squeeze x0 -> x1, local copies, waits for them, and re-layouts: none -> 1.41 us  [per_device(): return (both[0, :9], both[1, :9])]
where the time goes in v3:
time: 37.6 us; the launch traced here: 37.3 us
  Pallas kernels  35.3 us (94%)
  local copies, waits for them, and re-layouts  1.41 us (4%)
  between operations  0.64 us (2%)
    pallas_call x1, Pallas kernels, per_device(): pl.pallas_call(functools.partial(kernel, R, C), out_shape=jax.ShapeDtypeS...  35.3 us
    squeeze x1, local copies, waits for them, and re-layouts, per_device(): return (both[0, :9], both[1, :9])  1.41 us

profile of v3, /device:TPU:0, one launch (start us, length us, event | category | flops | bytes accessed | tf_op | source)
XLA Modules:
  0.0 37.3 jit_solution(10299185953637300388)
XLA Ops:
  0.6 35.3 %shard_map.68 = f32[2,16,512]{2,1,0:T(8,128)} custom-call(f32[8]{0:T(128)} %scale_in.1, f32[8,512]{1,0:T(8,128)} %points_in.1, f32[1,512]{1,0:T(1,128)} %bitcast.6, f32[1,512]{1,0:T(1,128)} %bitcast.7, s32[8,512]{1,0:T(8,128)} %bits_in.1), custom_call_target="tpu_custom_call" | custom-call | tf_op jit(solution)/shard_map/pallas_call | solution.py:329
  35.9 1.4 %slice_bitcast_fusion = (f32[9,512]{1,0:T(8,128)}, f32[9,512]{1,0:T(8,128)}) fusion(f32[2,16,512]{2,1,0:T(8,128)} %shard_map.68), kind=kLoop, calls=%fused_computation | loop fusion | bytes 73728 | tf_op jit(solution)/shard_map/squeeze | solution.py:359

commit v4 on v3

--- a/solution.py
+++ b/solution.py
@@ -155,7 +155,8 @@
             return carry
         lax.fori_loop(0, T, one, 0)
 
-    over_targets(lambda k: (copy_a(k).start(), copy_v(k).start()))
+    over_targets(lambda k: copy_a(k).start())
+    over_targets(lambda k: copy_v(k).start())
 
     @pl.when(in_group)
     def _():
@@ -197,19 +198,22 @@
     def first_of(t):
         return sixteen(slots_v[t, :, 0:n], slots_v[t, :, n:])
 
-    def step(k, accum):
+    def construct(k, carry):
         arrive(slots_a, recv_a, at(k), msg)
-        arrive(slots_v, recv_v, at(k - 1), msg_v)
-        accum = multiply(at(k - 1), halves(first_of(at(k - 1))), accum)
         build(at(k))
-        return accum
+        return carry
+
+    def gather(k, carry):
+        arrive(slots_v, recv_v, at(k), msg_v)
+        return carry
+
+    def product(t, accum):
+        return multiply(t, halves(first_of(t)), accum)
 
     zero = jnp.zeros((32, n), jnp.float32)
-    arrive(slots_a, recv_a, at(0), msg)
-    build(at(0))
-    accum = lax.fori_loop(1, G, step, zero)
-    arrive(slots_v, recv_v, at(G - 1), msg_v)
-    accum = multiply(at(G - 1), halves(first_of(at(G - 1))), accum)
+    lax.fori_loop(0, G, construct, 0)
+    lax.fori_loop(0, G, gather, 0)
+    accum = lax.fori_loop(0, G, product, zero, unroll=8)
 
     def across(phase, accum):
         parts[phase, me_c] = accum[0:16] + accum[16:32]

time: 37.6 us -> 35.3 us (0.939)
  Pallas kernels: 35.3 us -> 33 us
    pallas_call x1, Pallas kernels: 35.3 us -> 33 us  [per_device(): pl.pallas_call(functools.partial(kernel, R, C), out_shape=jax.ShapeDtypeS...]
where the time goes in v4:
time: 35.3 us; the launch traced here: 35.1 us
  Pallas kernels  33 us (93%)
  local copies, waits for them, and re-layouts  1.41 us (4%)
  between operations  0.64 us (2%)
    pallas_call x1, Pallas kernels, per_device(): pl.pallas_call(functools.partial(kernel, R, C), out_shape=jax.ShapeDtypeS...  33 us
    squeeze x1, local copies, waits for them, and re-layouts, per_device(): return (both[0, :9], both[1, :9])  1.41 us

profile of v4, /device:TPU:0, one launch (start us, length us, event | category | flops | bytes accessed | tf_op | source)
XLA Modules:
  0.0 35.1 jit_solution(5861985844557257390)
XLA Ops:
  0.6 33.0 %shard_map.68 = f32[2,16,512]{2,1,0:T(8,128)} custom-call(f32[8]{0:T(128)} %scale_in.1, f32[8,512]{1,0:T(8,128)} %points_in.1, f32[1,512]{1,0:T(1,128)} %bitcast.6, f32[1,512]{1,0:T(1,128)} %bitcast.7, s32[8,512]{1,0:T(8,128)} %bits_in.1), custom_call_target="tpu_custom_call" | custom-call | tf_op jit(solution)/shard_map/pallas_call | solution.py:333
  33.7 1.4 %slice_bitcast_fusion = (f32[9,512]{1,0:T(8,128)}, f32[9,512]{1,0:T(8,128)}) fusion(f32[2,16,512]{2,1,0:T(8,128)} %shard_map.68), kind=kLoop, calls=%fused_computation | loop fusion | bytes 73728 | tf_op jit(solution)/shard_map/squeeze | solution.py:363

commit v5 on v4

--- a/solution.py
+++ b/solution.py
@@ -246,9 +246,12 @@
 
     def send_image(k):
         copy_b(k).start()
+
+    def send_dots(k):
         for g in range(1, C):
             copy_s(k, g).start()
 
+    over_targets(send_dots)
     over_targets(send_image)
 
     @pl.when(in_group)

time: 35.3 us -> 34.8 us (0.986)
  Pallas kernels: 33 us -> 32.5 us
    pallas_call x1, Pallas kernels: 33 us -> 32.5 us  [per_device(): pl.pallas_call(functools.partial(kernel, R, C), out_shape=jax.ShapeDtypeS...]
where the time goes in v5:
time: 34.8 us; the launch traced here: 34.5 us
  Pallas kernels  32.5 us (93%)
  local copies, waits for them, and re-layouts  1.41 us (4%)
  between operations  0.64 us (2%)
    pallas_call x1, Pallas kernels, per_device(): pl.pallas_call(functools.partial(kernel, R, C), out_shape=jax.ShapeDtypeS...  32.5 us
    squeeze x1, local copies, waits for them, and re-layouts, per_device(): return (both[0, :9], both[1, :9])  1.41 us

profile of v5, /device:TPU:0, one launch (start us, length us, event | category | flops | bytes accessed | tf_op | source)
XLA Modules:
  0.0 34.5 jit_solution(11080849134601038778)
XLA Ops:
  0.6 32.5 %shard_map.68 = f32[2,16,512]{2,1,0:T(8,128)} custom-call(f32[8]{0:T(128)} %scale_in.1, f32[8,512]{1,0:T(8,128)} %points_in.1, f32[1,512]{1,0:T(1,128)} %bitcast.6, f32[1,512]{1,0:T(1,128)} %bitcast.7, s32[8,512]{1,0:T(8,128)} %bits_in.1), custom_call_target="tpu_custom_call" | custom-call | tf_op jit(solution)/shard_map/pallas_call | solution.py:336
  33.1 1.4 %slice_bitcast_fusion = (f32[9,512]{1,0:T(8,128)}, f32[9,512]{1,0:T(8,128)}) fusion(f32[2,16,512]{2,1,0:T(8,128)} %shard_map.68), kind=kLoop, calls=%fused_computation | loop fusion | bytes 73728 | tf_op jit(solution)/shard_map/squeeze | solution.py:366
